TPU v7x, 256 devices: a whole 4x4x8 slice. The times are simulated.
256 devices in a mesh: slot: 16 (over y, z_hi), head: 8 (over x, z_lo), blk: 2 (over core).
Axes of the slice: x: 4, y: 4, z: 8 (z_hi: 4, z_lo: 2; z = z_hi * 2 + z_lo), core: 2. Of those that a mesh axis runs over, the one named last changes fastest.
Arguments:
- query_rows: bfloat16 [16, 1024, 5120], P('slot', ('head', 'blk')), may hold values from -140 to 140
- key_rows: bfloat16 [16, 1024, 5120], P('slot', ('head', 'blk')), may hold values from -140 to 140
- value_rows: bfloat16 [16, 1024, 5120], P('slot', ('head', 'blk')), may hold values from -6 to 6
- query_gain: float32 [5120], replicated, may hold values from 0.1 to 1.9
- key_gain: float32 [5120], replicated, may hold values from 0.1 to 1.9
- out_weight: bfloat16 [5120, 5120], P('head', ('slot', 'blk')), may hold values from -0.5 to 0.5
- gate_table: float32 [50, 5120], replicated, may hold values from 0.5 to 3
- lengths: int32 [16], P('slot'), may hold values from 512 to 1024, as said below
- step_index: int32 [16], P('slot'), may hold values from 0 to 49
Outputs:
- attn_branch: bfloat16 [16, 1024, 5120], P('slot', ('head', 'blk'))
Inputs may be any that keep to these rules, and one draw needn't show every extreme that they name: `lengths`: some slot has half of 1024 valid tokens and another all 1024.
All inputs are finite; a program needn't handle non-finite values.
Results may differ from a plain program's by a relative error of at most 0.02.
Values may be sent and summed in bfloat16 or wider, within the bound.
A program may use at most 64 MiB of HBM per device.

v0:
```python
import math

import jax
import jax.numpy as jnp
from jax import lax
from jax.sharding import PartitionSpec as P

HD = 128


NEG_BIG = -1e30
EPSILON = 1e-06
KEY_BLOCK = 512


def rms_scaled(activations, gain_row):
    values = activations.astype(jnp.float32)
    mean_square = jnp.mean(values * values, axis=-1, keepdims=True)
    return (values * lax.rsqrt(mean_square + EPSILON) * gain_row).astype(jnp.bfloat16)


def fold_block(partial_value, queries, key_block, value_block, is_valid, head_dim):
    running_max, running_sum, weighted = partial_value
    local_heads = running_max.shape[0]
    q_split = queries.reshape(queries.shape[0], local_heads, head_dim)
    k_split = key_block.reshape(key_block.shape[0], local_heads, head_dim)
    v_split = value_block.reshape(value_block.shape[0], local_heads, head_dim)
    scores = jnp.einsum("qhd,khd->hqk", q_split, k_split, preferred_element_type=jnp.float32)
    scores = scores * (1.0 / math.sqrt(head_dim))
    keep_mask = is_valid[None, None, :]
    scores = jnp.where(keep_mask, scores, NEG_BIG)
    new_max = jnp.maximum(running_max, jnp.max(scores, axis=2))
    weights = jnp.where(keep_mask, jnp.exp(scores - new_max[:, :, None]), 0.0)
    rescale = jnp.exp(running_max - new_max)
    running_sum = running_sum * rescale + jnp.sum(weights, axis=2)
    update = jnp.einsum(
        "hqk,khd->hqd", weights.astype(jnp.bfloat16), v_split, preferred_element_type=jnp.float32
    )
    weighted = weighted * rescale[:, :, None] + update
    return (new_max, running_sum, weighted)


def fold_piece(partial_value, queries, key_piece, value_piece, where_at, length_limit, head_dim):
    row_count = key_piece.shape[0]
    block_rows = math.gcd(row_count, KEY_BLOCK)
    num_blocks = row_count // block_rows
    feature_width = key_piece.shape[1]
    blocks = (
        key_piece.reshape(num_blocks, block_rows, feature_width),
        value_piece.reshape(num_blocks, block_rows, feature_width),
        where_at.reshape(num_blocks, block_rows),
    )

    def advance(current, block_item):
        key_block, value_block, block_positions = block_item
        is_valid = block_positions < length_limit
        current = fold_block(current, queries, key_block, value_block, is_valid, head_dim)
        return (current, None)

    partial_value, unused = lax.scan(advance, partial_value, blocks)
    return partial_value


def positions_cycle(row_total, head_count, blk_count, tok_rows):
    index = jnp.arange(row_total, dtype=jnp.int32)
    per_blk = head_count * tok_rows
    source_blk = index // per_blk
    within = index % per_blk
    return (within // tok_rows * blk_count + source_blk) * tok_rows + within % tok_rows


def body(
    query_rows,
    key_rows,
    value_rows,
    query_gain,
    key_gain,
    out_weight,
    gate_table,
    lengths,
    step_index,
):
    tok_rows = query_rows.shape[1]
    model_width = query_rows.shape[2]
    head_count = lax.axis_size("head")
    blk_count = lax.axis_size("blk")
    head_dim = HD
    local_heads = model_width // head_count // head_dim
    length_limit = lengths[0]
    queries = rms_scaled(query_rows[0], query_gain)
    keys_normed = rms_scaled(key_rows[0], key_gain)
    values_local = value_rows[0]
    query_total = head_count * tok_rows
    start_state = (
        jnp.full((local_heads, query_total), NEG_BIG, jnp.float32),
        jnp.zeros((local_heads, query_total), jnp.float32),
        jnp.zeros((local_heads, query_total, head_dim), jnp.float32),
    )
    head_queries, head_keys, head_values = (
        lax.all_to_all(queries, "head", split_axis=1, concat_axis=0, tiled=True),
        lax.all_to_all(keys_normed, "head", split_axis=1, concat_axis=0, tiled=True),
        lax.all_to_all(values_local, "head", split_axis=1, concat_axis=0, tiled=True),
    )
    key_piece = lax.all_gather(head_keys, "blk", axis=0, tiled=True)
    value_piece = lax.all_gather(head_values, "blk", axis=0, tiled=True)
    where_at = positions_cycle(key_piece.shape[0], head_count, blk_count, tok_rows)
    finished = fold_piece(
        start_state, head_queries, key_piece, value_piece, where_at, length_limit, head_dim
    )
    running_max, running_sum, weighted = finished
    attended = (weighted / running_sum[:, :, None]).astype(jnp.bfloat16)
    attended = attended.transpose(1, 0, 2).reshape(query_total, local_heads * head_dim)
    full_columns = lax.all_gather(out_weight, ("slot", "blk"), axis=1, tiled=True)
    projected = lax.psum_scatter(
        jnp.dot(attended, full_columns, preferred_element_type=jnp.float32).astype(jnp.bfloat16),
        "head",
        scatter_dimension=0,
        tiled=True,
    ).astype(jnp.float32)
    step_rows = jnp.arange(gate_table.shape[0], dtype=jnp.int32)[:, None]
    gate_row = jnp.sum(jnp.where(step_rows == step_index[0], gate_table, 0.0), axis=0)
    return (gate_row * projected).astype(jnp.bfloat16)[None]


def solution(mesh):
    placed = (
        P("slot", ("head", "blk"), None),
        P("slot", ("head", "blk"), None),
        P("slot", ("head", "blk"), None),
        P(),
        P(),
        P("head", ("slot", "blk")),
        P(),
        P("slot"),
        P("slot"),
    )
    return jax.shard_map(
        body,
        mesh=mesh,
        in_specs=placed,
        out_specs=P("slot", ("head", "blk"), None),
        check_vma=False,
    )
```

profile of v0, /device:TPU:1, one launch (start us, length us, event | category | flops | bytes accessed | tf_op | source)
XLA Modules:
  0.0 263.2 jit_solution(3480364093095526069)
XLA Ops:
  6.5 1.3 multiply_reduce_fusion.1
  7.9 1.2 copy.57
  9.4 16.9 %all_to_all.51 = bf16[64,8,640]{2,0,1:T(8,128)(2,1)} all-to-all(bf16[64,8,640]{2,0,1:T(8,128)(2,1)S(1)} %copy.44), channel_id=1, replica_groups=mesh['slot'=16,'head'=8,'blk'=2] {'head'}, dimensions={1} | all-to-all | bytes 1310720 | tf_op jit(solution)/shard_map/all_to_all | solution.py:101
  26.5 12.7 %all_to_all.52 = bf16[64,8,640]{2,0,1:T(8,128)(2,1)} all-to-all(bf16[64,8,640]{2,0,1:T(8,128)(2,1)S(1)} %copy.46), channel_id=1, replica_groups=mesh['slot'=16,'head'=8,'blk'=2] {'head'}, dimensions={1} | all-to-all | bytes 1310720 | tf_op jit(solution)/shard_map/all_to_all | solution.py:102
  41.5 3.5 %all-to-all-start.1 = ((bf16[64,8,640]{2,0,1:T(8,128)(2,1)}), bf16[64,8,640]{2,0,1:T(8,128)(2,1)S(1)}, u32[]{:S(2)}, u32[]{:S(2)}) async-start(bf16[64,8,640]{2,0,1:T(8,128)(2,1)} %copy.45), calls=%async_computation.1 | async-start | bytes 1310720 | tf_op jit(solution)/shard_map/all_to_all | solution.py:100
  45.2 8.2 %all-to-all-done.1 = bf16[64,8,640]{2,0,1:T(8,128)(2,1)S(1)} async-done(((bf16[64,8,640]{2,0,1:T(8,128)(2,1)}), bf16[64,8,640]{2,0,1:T(8,128)(2,1)S(1)}, u32[]{:S(2)}, u32[]{:S(2)}) %all-to-all-start.1) | async-done | bytes 655392 | tf_op jit(solution)/shard_map/all_to_all | solution.py:100
  53.6 7.7 %all-gather.6.cloned.1.call-done = bf16[1024,640]{1,0:T(8,128)(2,1)} async-done(((bf16[512,640]{1,0:T(8,128)(2,1)}), bf16[1024,640]{1,0:T(8,128)(2,1)}) %all-gather.6.cloned.1.call-update) | async-done | bytes 1310736 | tf_op jit(solution)/shard_map/all_gather | solution.py:105
  61.3 32.9 %while.15 = (s32[]{:T(128)}, f32[5,512]{1,0:T(8,128)S(1)}, f32[5,512]{1,0:T(8,128)S(1)}, f32[5,512,128]{2,1,0:T(8,128)}, s32[2,512]{1,0:T(2,128)S(1)}, /*index=5...) while((s32[]{:T(128)}, f32[5,512]{1,0:T(8,128)S(1)}, ...), condition=%wide.region_6.7_spmd.clone, body=%wide.region_3.6_spmd.clone.sunk | while | flops 689124352 | bytes 36212924 | solution.py:60
  62.0 1.4 constant_dynamic-slice_fusion.3
  63.6 3.7 %bitcast_reduce_fusion.2 = (f32[5,512]{1,0:T(8,128)S(1)}, f32[5,512,512]{2,1,0:T(8,128)}) fusion(pred[512]{0:T(512)(128)(4,1)S(1)} %compare_reduce_fusion.2, bf16[512,5,128]{0,2,1:T(8,128)(2,1)S(1)} %bitcast.80, bf16[512,5,128]{0,2,1:T(8,128)(2,1)S(1)} %bitcast.81), kind=kOutput, calls=%fused_computation.1.clone.1 | convolution fusion | flops 339473920 | bytes 6564352 | tf_op jit(solution)/shard_map/while/body/eval_jaxpr/qhd,khd->hqk/dot_general | solution.py:28
  67.3 3.3 %fusion.38 = f32[5,512]{1,0:T(8,128)S(1)} fusion(f32[5,512,512]{2,1,0:T(8,128)} %get-tuple-element.199, f32[5,512]{1,0:T(8,128)S(1)} %select_maximum_fusion.2, pred[512]{0:T(512)(128)(4,1)S(1)} %compare_reduce_fusion.2), kind=kLoop, calls=%fused_computation.6.clone.1 | loop fusion | flops 6551040 | bytes 5263872 | tf_op jit(solution)/shard_map/while/body/eval_jaxpr/reduce_sum | solution.py:35
  71.9 4.7 %fusion.40 = f32[5,512,128]{2,1,0:T(8,128)S(1)} fusion(bf16[512,5,128]{0,2,1:T(8,128)(2,1)S(1)} %bitcast.82, f32[5,512,512]{2,1,0:T(8,128)} %get-tuple-element.199, f32[5,512]{1,0:T(8,128)S(1)} %select_maximum_fusion.2, pred[512]{0:T(512)(128)(4,1)S(1)} %compare_reduce_fusion.2, f32[5,512,128]{2,1,0:T(8,128)S(1)} %copy-done.1, ...), kind=kOutput, calls=%fused_computation.10.clone.1 | convolution fusion | flops 343080960 | bytes 8540673 | tf_op jit(solution)/shard_map/while/body/eval_jaxpr/hqk,khd->hqd/dot_general | solution.py:36
  76.7 1.0 copy-done.2
  78.4 1.4 constant_dynamic-slice_fusion.3
  80.1 3.7 %bitcast_reduce_fusion.2 = (f32[5,512]{1,0:T(8,128)S(1)}, f32[5,512,512]{2,1,0:T(8,128)}) fusion(pred[512]{0:T(512)(128)(4,1)S(1)} %compare_reduce_fusion.2, bf16[512,5,128]{0,2,1:T(8,128)(2,1)S(1)} %bitcast.80, bf16[512,5,128]{0,2,1:T(8,128)(2,1)S(1)} %bitcast.81), kind=kOutput, calls=%fused_computation.1.clone.1 | convolution fusion | flops 339473920 | bytes 6564352 | tf_op jit(solution)/shard_map/while/body/eval_jaxpr/qhd,khd->hqk/dot_general | solution.py:28
  83.7 3.3 %fusion.38 = f32[5,512]{1,0:T(8,128)S(1)} fusion(f32[5,512,512]{2,1,0:T(8,128)} %get-tuple-element.199, f32[5,512]{1,0:T(8,128)S(1)} %select_maximum_fusion.2, pred[512]{0:T(512)(128)(4,1)S(1)} %compare_reduce_fusion.2), kind=kLoop, calls=%fused_computation.6.clone.1 | loop fusion | flops 6551040 | bytes 5263872 | tf_op jit(solution)/shard_map/while/body/eval_jaxpr/reduce_sum | solution.py:35
  87.4 1.0 copy-done.1
  88.4 4.7 %fusion.40 = f32[5,512,128]{2,1,0:T(8,128)S(1)} fusion(bf16[512,5,128]{0,2,1:T(8,128)(2,1)S(1)} %bitcast.82, f32[5,512,512]{2,1,0:T(8,128)} %get-tuple-element.199, f32[5,512]{1,0:T(8,128)S(1)} %select_maximum_fusion.2, pred[512]{0:T(512)(128)(4,1)S(1)} %compare_reduce_fusion.2, f32[5,512,128]{2,1,0:T(8,128)S(1)} %copy-done.1, ...), kind=kOutput, calls=%fused_computation.10.clone.1 | convolution fusion | flops 343080960 | bytes 8540673 | tf_op jit(solution)/shard_map/while/body/eval_jaxpr/hqk,khd->hqd/dot_general | solution.py:36
  93.2 1.0 copy-done.2
  94.2 1.7 copy.50
  96.1 38.8 %all-gather.8.cloned.1.call-done = bf16[640,5120]{0,1:T(8,128)(2,1)} async-done(((bf16[640,160]{0,1:T(8,128)(2,1)}), bf16[640,5120]{0,1:T(8,128)(2,1)}) %all-gather.8.cloned.1.call-update) | async-done | bytes 6553616 | tf_op jit(solution)/shard_map/all_gather | solution.py:113
  135.0 8.9 %convolution_convert_fusion = bf16[512,5120]{1,0:T(8,128)(2,1)} fusion(bf16[512,640]{0,1:T(8,128)(2,1)S(1)} %bitcast.92, bf16[640,5120]{0,1:T(8,128)(2,1)} %all-gather.8.cloned.1.call-done), kind=kOutput, calls=%fused_computation.22 | convolution fusion | flops 3358064640 | bytes 12451840 | tf_op jit(solution)/shard_map/dot_general | solution.py:115
  145.4 109.3 %reduce-scatter.2.cloned.1.call-done = bf16[64,5120]{1,0:T(8,128)(2,1)} async-done(((bf16[512,5120]{1,0:T(8,128)(2,1)}), bf16[64,5120]{1,0:T(8,128)(2,1)}) %reduce-scatter.2.cloned.1.call-update) | async-done | bytes 655376 | tf_op jit(solution)/shard_map/reduce_scatter | solution.py:114
  254.7 2.0 fusion.19
  (56 shorter events, 7.4 us)
Async XLA Ops:
  6.5 2.5 copy-start.5
  6.5 47.1 %all-gather.4.cloned.1.call-start = ((), (), s32[]{:S(2)}) async-start(), calls=%async_computation.4 | async-start | bytes 1966080 | tf_op jit(solution)/shard_map/all_gather | solution.py:104
  9.4 16.9 %copy-start.4 = (bf16[1,64,5120]{2,1,0:T(8,128)(2,1)S(1)}, bf16[1,64,5120]{2,1,0:T(8,128)(2,1)}, u32[]{:S(2)}) copy-start(bf16[1,64,5120]{2,1,0:T(8,128)(2,1)} %param.13) | copy-start | bytes 1966084
  26.3 35.0 %all-gather.6.cloned.1.call-start = ((), (), s32[]{:S(2)}) async-start(), calls=%async_computation.5 | async-start | bytes 1966080 | tf_op jit(solution)/shard_map/all_gather | solution.py:105
  26.5 13.5 %copy-start = (bf16[1,64,5120]{2,1,0:T(8,128)(2,1)S(1)}, bf16[1,64,5120]{2,1,0:T(8,128)(2,1)}, u32[]{:S(2)}) copy-start(bf16[1,64,5120]{2,1,0:T(8,128)(2,1)} %param.11) | copy-start | bytes 1966084
  39.2 0.9 copy-start.6
  39.3 95.7 %all-gather.8.cloned.1.call-start = ((), (), s32[]{:S(2)}) async-start(), calls=%async_computation.6 | async-start | bytes 6758400 | tf_op jit(solution)/shard_map/all_gather | solution.py:113
  41.5 11.8 %all-to-all-start.1 = ((bf16[64,8,640]{2,0,1:T(8,128)(2,1)}), bf16[64,8,640]{2,0,1:T(8,128)(2,1)S(1)}, u32[]{:S(2)}, u32[]{:S(2)}) async-start(bf16[64,8,640]{2,0,1:T(8,128)(2,1)} %copy.45), calls=%async_computation.1 | async-start | bytes 1310720 | tf_op jit(solution)/shard_map/all_to_all | solution.py:100
  45.0 209.6 %reduce-scatter.2.cloned.1.call-start = ((), (), s32[]{:S(2)}) async-start(), calls=%async_computation.7 | async-start | bytes 5898240 | tf_op jit(solution)/shard_map/reduce_scatter | solution.py:114
  70.6 1.3 copy-start.1
  76.7 1.1 copy-start.2
  87.1 1.3 copy-start.1
  93.2 1.1 copy-start.2
  143.9 1.3 copy-start.3
Sparse Core Ops, SparseCore 0:
  26.4 16.9 all-gather.3
  45.2 16.0 all-gather.5
  63.8 71.0 all-gather.7
  144.0 110.5 reduce-scatter.1
where the time goes:
time: 264 us; the launch traced here: 263 us
  waiting for transfers between devices  165 us (62%)
  blocking collectives  29.6 us (11%)
  matrix products  25.7 us (10%)
  between operations  14.1 us (5%)
  local copies, waits for them, and re-layouts  12.9 us (5%)
  other arithmetic  12.4 us (5%)
  starting transfers between devices  3.67 us (1%)
    reduce_scatter x1, waiting for transfers between devices, body(): lax.psum_scatter(jnp.dot(attended, full_columns, preferred_element_type=j...  109 us
    all_gather x1, waiting for transfers between devices, body(): lax.all_gather(out_weight, ('slot', 'blk'), axis=1, tiled=True)  38.8 us
    all_to_all x1, blocking collectives, body(): lax.all_to_all(keys_normed, 'head', split_axis=1, concat_axis=0, tiled=True)  16.9 us
    all_to_all x1, blocking collectives, body(): lax.all_to_all(values_local, 'head', split_axis=1, concat_axis=0, tiled=T...  12.7 us
    dot_general x2, matrix products, fold_block(): jnp.einsum('hqk,khd->hqd', weights.astype(jnp.bfloat16), v_split, preferr...  9.45 us
    dot_general x1, matrix products, body(): jnp.dot(attended, full_columns, preferred_element_type=jnp.float32)  8.94 us
    all_to_all x1, waiting for transfers between devices, body(): lax.all_to_all(queries, 'head', split_axis=1, concat_axis=0, tiled=True)  8.16 us
    all_gather x1, waiting for transfers between devices, body(): value_piece = lax.all_gather(head_values, 'blk', axis=0, tiled=True)  7.68 us
  transfers between devices with their start and end apart: 5, of which 4 were waited for; matrix products, arithmetic and copies ran while one was open for 12% of the time, Pallas kernels for 0%

commit v1 on v0

v1 whole, which is shorter than its diff:
```python
import functools
import math

import jax
import jax.numpy as jnp
from jax import lax
from jax.experimental import pallas as pl
from jax.experimental.pallas import tpu as pltpu
from jax.sharding import PartitionSpec as P

HD = 128
NEG_BIG = -1e30
EPSILON = 1e-06
MESH = pl.DeviceIdType.MESH

NX, NY, NZ, NC = 4, 4, 8, 2
TOK = 64
D = 5120
GW = 640
LOCAL_HEADS = GW // HD
KEYS = 1024
WC = 160
GC = 2 * WC
GROUPS = 8
STEPS = 50
BF = jnp.bfloat16
F32 = jnp.float32


def al(value, unit):
    return pl.multiple_of(value, unit)


def kernel(
    len_ref, step_ref, q_hbm, k_hbm, v_hbm, qg_ref, kg_ref, w_hbm, gt_hbm, out_hbm,
    q_raw, k_raw, q_nrm, k_nrm, w_raw, w_own, gate_tab, gate_row, qb, kb, vb, bias, wt,
    a_stage, at, pf, far_out, far_in, near_out, near_in, ft, ob,
    ld, qs, qr, ks, kr, vs, vr, fs, fr, w0s, w0r, zs, zr, yds, ydr, yrs, yrr,
    azs, azr, aos, aor, afs, afr, ffs, ffr, nns, nnr, fins, finr, finl,
):
    slot = lax.axis_index("slot")
    head = lax.axis_index("head")
    c = lax.axis_index("blk")
    x, zl = head // 2, head % 2
    y, zh = slot // 4, slot % 4
    z = zh * 2 + zl
    oc = 1 - c
    row_core = y // 2
    is_row_core = c == row_core

    def dev(dx, dy, dz, dc):
        return (dy * 4 + dz // 2, dx * 2 + dz % 2, dc)

    def rc(src, dst, send, recv, device):
        return pltpu.make_async_remote_copy(
            src_ref=src, dst_ref=dst, send_sem=send, recv_sem=recv,
            device_id=device, device_id_type=MESH,
        )

    def got(ref, sem):
        pltpu.make_async_copy(ref, ref, sem).wait()

    xp, xm = (x + 1) % NX, (x + 3) % NX
    yp, ym = (y + 1) % NY, (y + 3) % NY
    zp, zm = (z + 1) % NZ, (z + 7) % NZ
    z_mate = zh * 2 + (1 - zl)
    z_out = (z + NZ - 1 + 2 * zl) % NZ
    other = dev(x, y, z, oc)

    load_w = pltpu.make_async_copy(w_hbm, w_raw, ld.at[0])
    load_k = pltpu.make_async_copy(k_hbm.at[0], k_raw, ld.at[1])
    load_q = pltpu.make_async_copy(q_hbm.at[0], q_raw, ld.at[2])
    load_g = pltpu.make_async_copy(
        gt_hbm.at[:, pl.ds(al(c * 2560, 128), 2560)], gate_tab, ld.at[3]
    )
    load_w.start()
    load_k.start()
    load_q.start()
    load_g.start()

    barrier = pltpu.get_barrier_semaphore()
    partners = []
    for dh in range(8):
        for dc in range(2):
            if (dh, dc) != (0, 0):
                ph = (head + dh) % 8
                partners.append((slot, ph, (c + dc) % 2))
    for dc in range(2):
        partners.append(dev(x, y, z_out, dc))
        partners.append(dev(x, yp, z, dc))
        partners.append(dev(x, ym, z, dc))
    for partner in partners:
        pl.semaphore_signal(barrier, inc=1, device_id=partner, device_id_type=MESH)
    pl.semaphore_wait(barrier, len(partners))

    def cols(ref, group):
        return ref.at[:, pl.ds(al(group * GW, 128), GW)]

    def kv_place(buf, which_c, src_head):
        return buf.at[pl.ds(al(which_c * 512 + src_head * TOK, TOK), TOK), :]

    def kv_send(src, buf, send, recv):
        pltpu.make_async_copy(cols(src, head), kv_place(buf, c, head), recv.at[head]).start()

        def one(t, carry):
            group = (head + t) % 8
            rc(cols(src, group), kv_place(buf, c, head), send.at[group], recv.at[head],
               (slot, group, c)).start()
            return carry
        lax.fori_loop(1, 8, one, 0)

    def kv_send_wait(src, buf, send, recv):
        def one(t, carry):
            group = (head + t) % 8
            rc(cols(src, group), kv_place(buf, c, head), send.at[group], recv.at[head],
               (slot, group, c)).wait_send()
            return carry
        lax.fori_loop(1, 8, one, 0)

    def kv_forward(buf, recv, index):
        def one(t, carry):
            got(kv_place(buf, c, t), recv.at[t])
            return carry
        lax.fori_loop(0, 8, one, 0)
        half = buf.at[pl.ds(al(c * 512, 512), 512), :]
        rc(half, half, fs.at[index], fr.at[index], other).start()

    kv_send(v_hbm.at[0], vb, vs, vr)

    def piece(ys, zs_, half=None):
        row = ((ys % 2) * 4 + zs_ // 2) * GC
        size = GC
        if half is not None:
            row = row + half * WC
            size = WC
        return wt.at[pl.ds(al(row, 32), size), pl.ds(al((zs_ % 2) * GW, 128), GW)]

    load_w.wait()
    w_own[...] = w_raw[...].astype(F32).T.astype(BF)

    @pl.when(is_row_core)
    def _():
        pltpu.make_async_copy(w_own, piece(y, z, c), w0r.at[c]).start()

    @pl.when(jnp.logical_not(is_row_core))
    def _():
        rc(w_own, piece(y, z, c), w0s, w0r.at[c], other).start()

    def row_sends(zsrc, j):
        for d, yt in ((0, yp), (1, ym)):
            yield rc(piece(y, zsrc), piece(y, zsrc), yds.at[d, j], ydr.at[j],
                     dev(x, yt, z, row_core))

    def z_send(d, k):
        zsrc = (z + NZ - (k - 1)) % NZ if d == 0 else (z + k - 1) % NZ
        half = None if k < 4 else d
        return rc(piece(y, zsrc, half), piece(y, zsrc, half), zs.at[d, k - 1], zr.at[d, k - 1],
                  dev(x, y, zp if d == 0 else zm, row_core))

    def z_from(d, k):
        return (z + NZ - k) % NZ if d == 0 else (z + k) % NZ

    def z_index(d, k):
        ahead = zl if d == 0 else 1 - zl
        if k == 1:
            return 2 - ahead
        if k == 2:
            return 3 + ahead
        return 6 - ahead

    def z_first():
        @pl.when(is_row_core)
        def _():
            got(piece(y, z, 0), w0r.at[0])
            got(piece(y, z, 1), w0r.at[1])
            for d in range(2):
                z_send(d, 1).start()
            for cp in row_sends(z, 0):
                cp.start()

    def z_service(k):
        @pl.when(is_row_core)
        def _():
            for d in range(2):
                zsrc = z_from(d, k)
                got(piece(y, zsrc), zr.at[d, k - 1])
                z_send(d, k + 1).start()
                for cp in row_sends(zsrc, z_index(d, k)):
                    cp.start()

    def z_last():
        @pl.when(is_row_core)
        def _():
            zsrc = (z + 4) % NZ
            for d in range(2):
                got(piece(y, zsrc, d), zr.at[d, 3])
            for cp in row_sends(zsrc, 7):
                cp.start()

    from_plus = ((y + 1) % 2) * (1 - (c - row_core) * (c - row_core)) + (y % 2) * (
        (c - row_core) * (c - row_core))
    direct_row = (y + 3 + 2 * from_plus) % NY
    relay_to = (y + 1 + 2 * from_plus) % NY
    sgn = 1 - 2 * zl
    DELTA = (0, 1, -1, -2, 2, 3, -3, 4)

    def z_of(j):
        return (z + NZ + sgn * DELTA[j]) % NZ

    def relay(j):
        zsrc = z_of(j)
        ref = piece(direct_row, zsrc, from_plus)
        return rc(ref, ref, yrs.at[j], yrr.at[from_plus, j], dev(x, relay_to, z, c))

    def y_service(j):
        got(piece(direct_row, z_of(j)), ydr.at[j])
        relay(j).start()

    z_first()

    def norm(raw, gain_ref, out):
        def rows(i, carry):
            here = pl.ds(al(i * 16, 16), 16)
            vals = raw[here, :].astype(F32)
            mean_square = jnp.mean(vals * vals, axis=-1, keepdims=True)
            out[here, :] = (vals * lax.rsqrt(mean_square + EPSILON) * gain_ref[...]).astype(BF)
            return carry
        lax.fori_loop(0, TOK // 16, rows, 0)

    load_k.wait()
    norm(k_raw, kg_ref, k_nrm)
    kv_send(k_nrm, kb, ks, kr)
    load_q.wait()
    norm(q_raw, qg_ref, q_nrm)

    q_core = x // 2

    def q_place(src_x, src_zl, src_c):
        row = src_zl * 256 + (src_x % 2) * 128 + src_c * TOK
        return qb.at[pl.ds(al(row, TOK), TOK), :]

    q_index = (x % 2) * 4 + zl * 2 + c
    q_stays = c == q_core

    @pl.when(q_stays)
    def _():
        pltpu.make_async_copy(cols(q_nrm, head), q_place(x, zl, c), qr.at[q_index]).start()

    def q_copy(group):
        return rc(cols(q_nrm, group), q_place(x, zl, c), qs.at[group], qr.at[q_index],
                  (slot, group, q_core))

    @pl.when(jnp.logical_not(q_stays))
    def _():
        q_copy(head).start()

    def q_send(t, carry):
        q_copy((head + t) % 8).start()
        return carry
    lax.fori_loop(1, 8, q_send, 0)

    def mask_rows(i, carry):
        row = lax.broadcasted_iota(jnp.int32, (TOK, 128), 0)
        pos = (i % 8) * 128 + (i // 8) * TOK + row
        bias[pl.ds(al(i * TOK, TOK), TOK), :] = jnp.where(pos < len_ref[0], 0.0, NEG_BIG)
        return carry
    lax.fori_loop(0, KEYS // TOK, mask_rows, 0)

    load_g.wait()
    step_rows = lax.broadcasted_iota(jnp.int32, (STEPS, 2560), 0)
    gate_row[...] = jnp.sum(
        jnp.where(step_rows == step_ref[0], gate_tab[...], 0.0), axis=0, keepdims=True)

    z_service(1)
    kv_forward(vb, vr, 0)
    y_service(0)
    z_service(2)
    kv_forward(kb, kr, 1)
    y_service(1)
    z_service(3)

    def q_wait(t, carry):
        got(qb.at[pl.ds(al((t // 2 % 2) * 256 + (t // 4) * 128 + (t % 2) * TOK, TOK), TOK), :],
            qr.at[t])
        return carry
    lax.fori_loop(0, 8, q_wait, 0)
    for buf, index in ((vb, 0), (kb, 1)):
        got(buf.at[pl.ds(al(oc * 512, 512), 512), :], fr.at[index])

    scale = math.log2(math.e) / math.sqrt(HD)
    mine = pl.ds(al(c * 256, 128), 256)
    theirs = pl.ds(al(oc * 256, 128), 256)

    def feats(which_zl, hh):
        return pl.ds(al(which_zl * GW + hh * HD, HD), HD)

    def attend(hh, zq):
        lanes = pl.ds(al(hh * HD, HD), HD)
        keys = kb[:, lanes]
        queries = qb[pl.ds(al(zq * 256, 256), 256), lanes]
        scores = lax.dot_general(keys, queries, (((1,), (1,)), ((), ())),
                                 preferred_element_type=F32)
        scores = scores * scale + jnp.concatenate([bias[...], bias[...]], axis=1)
        top = jnp.max(scores, axis=0, keepdims=True)
        weights = jnp.exp2(scores - top)
        total = jnp.sum(weights, axis=0, keepdims=True)
        mixed = lax.dot_general(vb[:, lanes], weights.astype(BF), (((0,), (0,)), ((), ())),
                                preferred_element_type=F32)
        return (mixed / total).astype(BF)

    def away_copy(hh):
        return rc(a_stage.at[hh], at.at[feats(zl, hh), mine], azs.at[hh], azr.at[hh],
                  dev(x, y, z_mate, c))

    def home_copy(hh):
        ref = at.at[feats(zl, hh), mine]
        return rc(ref, ref, aos.at[hh], aor.at[hh], other)

    def pass_copy(hh):
        ref = at.at[feats(1 - zl, hh), mine]
        return rc(ref, ref, afs.at[hh], afr.at[hh], other)

    def one_head(hh, carry):
        a_stage[hh] = attend(hh, 1 - zl)
        away_copy(hh).start()
        at[feats(zl, hh), mine] = attend(hh, zl)
        home_copy(hh).start()
        return carry
    lax.fori_loop(0, 2, one_head, 0)
    y_service(2)
    z_last()
    lax.fori_loop(2, 4, one_head, 0)
    y_service(3)
    lax.fori_loop(4, 5, one_head, 0)

    def pass_on(hh, carry):
        got(at.at[feats(1 - zl, hh), mine], azr.at[hh])
        pass_copy(hh).start()
        return carry
    lax.fori_loop(0, LOCAL_HEADS, pass_on, 0)

    def attended_wait(hh, carry):
        got(at.at[feats(zl, hh), theirs], aor.at[hh])
        got(at.at[feats(1 - zl, hh), theirs], afr.at[hh])
        return carry
    lax.fori_loop(0, LOCAL_HEADS, attended_wait, 0)

    own = 1 - (c - row_core) * (c - row_core)

    def group_of(i):
        pair = own * (i % 4) + (1 - own) * (i // 2)
        first = own * (1 - i // 4) + (1 - own) * (1 - i % 2)
        row = own * (first * y + (1 - first) * direct_row) + (1 - own) * (
            first * direct_row + (1 - first) * ((y + 2) % NY))
        is1 = (pair % 2) * (1 - pair // 2)
        is2 = (1 - pair % 2) * (pair // 2)
        is3 = (pair % 2) * (pair // 2)
        gz = (zh + 4 - sgn * is1 + sgn * is2 + 2 * is3) % 4
        return (row % 2) * 4 + gz

    def far_wait_pair(p):
        @pl.when(jnp.logical_not(is_row_core))
        def _():
            for j in (2 * p, 2 * p + 1):
                for half in range(2):
                    got(piece((y + 2) % NY, z_of(j), half), yrr.at[half, j])

    def lane_block(xx):
        return pl.ds(al(xx * 128, 128), 128)

    def far_copies(i):
        yield rc(far_out.at[i, pl.ds(0, WC), :], far_in.at[i, 0], ffs.at[i, 0], ffr.at[i, 0],
                 dev(xp, y, z, c))
        yield rc(far_out.at[i, pl.ds(WC, WC), :], far_in.at[i, 1], ffs.at[i, 1], ffr.at[i, 1],
                 dev(xm, y, z, c))

    def near_copies(i):
        yield rc(near_out.at[i, 0], near_in.at[i, 0], nns.at[i, 0], nnr.at[i, 0], dev(xp, y, z, c))
        yield rc(near_out.at[i, 1], near_in.at[i, 1], nns.at[i, 1], nnr.at[i, 1], dev(xm, y, z, c))

    def stage_a(i):
        slot_i = i % 3
        rows = pl.ds(al(group_of(i) * GC, 32), GC)
        pf[slot_i] = jnp.dot(wt[rows, :], at[...], preferred_element_type=F32)
        far_out[i] = pf[slot_i, :, lane_block((x + 2) % NX)].astype(BF)
        for cp in far_copies(i):
            cp.start()

    def stage_b(i):
        slot_i = i % 3
        for d in range(2):
            got(far_in.at[i, d], ffr.at[i, d])
        up = lane_block(xp)
        down = lane_block(xm)
        lo, hi = pl.ds(0, WC), pl.ds(WC, WC)
        near_out[i, 0, lo, :] = (pf[slot_i, lo, up] + far_in[i, 0].astype(F32)).astype(BF)
        near_out[i, 0, hi, :] = pf[slot_i, hi, up].astype(BF)
        near_out[i, 1, lo, :] = pf[slot_i, lo, down].astype(BF)
        near_out[i, 1, hi, :] = (pf[slot_i, hi, down] + far_in[i, 1].astype(F32)).astype(BF)
        for cp in near_copies(i):
            cp.start()

    def stage_c(i):
        slot_i = i % 3
        for d in range(2):
            got(near_in.at[i, d], nnr.at[i, d])
        rows = pl.ds(al(group_of(i) * GC, 32), GC)
        ft[rows, :] = (pf[slot_i, :, lane_block(x)] + near_in[i, 0].astype(F32)
                       + near_in[i, 1].astype(F32))

    def step(i, carry):
        @pl.when(i == 2)
        def _():
            y_service(4)

        @pl.when(i == 4)
        def _():
            y_service(5)

        @pl.when(i == 5)
        def _():
            y_service(6)

        @pl.when(i == 6)
        def _():
            y_service(7)
        for p in range(4):
            @pl.when(i == 2 * p + 1)
            def _(p=p):
                far_wait_pair(p)

        @pl.when(i < GROUPS)
        def _():
            stage_a(i)

        @pl.when(jnp.logical_and(i >= 1, i < GROUPS + 1))
        def _():
            stage_b(i - 1)

        @pl.when(i >= 2)
        def _():
            stage_c(i - 2)
        return carry
    lax.fori_loop(0, GROUPS + 2, step, 0)

    def finish(b, carry):
        here = pl.ds(al(b * 128, 128), 128)
        ob[:, here] = (ft[here, :].T * gate_row[:, here]).astype(BF)
        return carry
    lax.fori_loop(0, 20, finish, 0)
    half_cols = pl.ds(al(c * 2560, 128), 2560)
    keep = pltpu.make_async_copy(
        ob.at[pl.ds(al(c * TOK, TOK), TOK), :], out_hbm.at[0, :, half_cols], finl)
    keep.start()
    give = rc(ob.at[pl.ds(al(oc * TOK, TOK), TOK), :], out_hbm.at[0, :, half_cols], fins, finr,
              other)
    give.start()

    kv_send_wait(v_hbm.at[0], vb, vs, vr)
    kv_send_wait(k_nrm, kb, ks, kr)

    def q_sent(t, carry):
        q_copy((head + t) % 8).wait_send()
        return carry
    lax.fori_loop(1, 8, q_sent, 0)

    @pl.when(jnp.logical_not(q_stays))
    def _():
        q_copy(head).wait_send()
    for buf, index in ((vb, 0), (kb, 1)):
        half = buf.at[pl.ds(al(c * 512, 512), 512), :]
        rc(half, half, fs.at[index], fr.at[index], other).wait_send()

    @pl.when(jnp.logical_not(is_row_core))
    def _():
        rc(w_own, piece(y, z, c), w0s, w0r.at[c], other).wait_send()

    @pl.when(is_row_core)
    def _():
        for d in range(2):
            for k in range(1, 5):
                z_send(d, k).wait_send()
        for cp in row_sends(z, 0):
            cp.wait_send()
        for k in range(1, 4):
            for d in range(2):
                for cp in row_sends(z_from(d, k), z_index(d, k)):
                    cp.wait_send()
        for cp in row_sends((z + 4) % NZ, 7):
            cp.wait_send()
    for j in range(8):
        relay(j).wait_send()

    def heads_sent(hh, carry):
        away_copy(hh).wait_send()
        home_copy(hh).wait_send()
        pass_copy(hh).wait_send()
        return carry
    lax.fori_loop(0, LOCAL_HEADS, heads_sent, 0)

    def sums_sent(i, carry):
        for cp in far_copies(i):
            cp.wait_send()
        for cp in near_copies(i):
            cp.wait_send()
        return carry
    lax.fori_loop(0, GROUPS, sums_sent, 0)
    keep.wait()
    give.wait_send()
    got(out_hbm.at[0, :, pl.ds(al(oc * 2560, 128), 2560)], finr)


def body(query_rows, key_rows, value_rows, query_gain, key_gain, out_weight, gate_table, lengths,
         step_index):
    vmem = pl.BlockSpec(memory_space=pltpu.VMEM)
    smem = pl.BlockSpec(memory_space=pltpu.SMEM)
    hbm = pl.BlockSpec(memory_space=pl.ANY)
    sem = pltpu.SemaphoreType.DMA
    flops = 2 * (2 * 5 * 512 * 1024 * 128 + 512 * 1280 * 2560)
    return pl.pallas_call(
        kernel,
        out_shape=jax.ShapeDtypeStruct((1, TOK, D), BF),
        in_specs=[smem, smem, hbm, hbm, hbm, vmem, vmem, hbm, hbm],
        out_specs=hbm,
        scratch_shapes=[
            pltpu.VMEM((TOK, D), BF),
            pltpu.VMEM((TOK, D), BF),
            pltpu.VMEM((TOK, D), BF),
            pltpu.VMEM((TOK, D), BF),
            pltpu.VMEM((GW, WC), BF),
            pltpu.VMEM((WC, GW), BF),
            pltpu.VMEM((STEPS, 2560), F32),
            pltpu.VMEM((1, 2560), F32),
            pltpu.VMEM((512, GW), BF),
            pltpu.VMEM((KEYS, GW), BF),
            pltpu.VMEM((KEYS, GW), BF),
            pltpu.VMEM((KEYS, 128), F32),
            pltpu.VMEM((2560, 2 * GW), BF),
            pltpu.VMEM((LOCAL_HEADS, HD, 256), BF),
            pltpu.VMEM((2 * GW, 512), BF),
            pltpu.VMEM((3, GC, 512), F32),
            pltpu.VMEM((GROUPS, GC, 128), BF),
            pltpu.VMEM((GROUPS, 2, WC, 128), BF),
            pltpu.VMEM((GROUPS, 2, GC, 128), BF),
            pltpu.VMEM((GROUPS, 2, GC, 128), BF),
            pltpu.VMEM((2560, 128), F32),
            pltpu.VMEM((128, 2560), BF),
            sem((4,)),
            sem((8,)), sem((8,)), sem((8,)), sem((8,)), sem((8,)), sem((8,)),
            sem((2,)), sem((2,)),
            sem, sem((2,)),
            sem((2, 4)), sem((2, 4)),
            sem((2, 8)), sem((8,)),
            sem((8,)), sem((2, 8)),
            sem((5,)), sem((5,)), sem((5,)), sem((5,)), sem((5,)), sem((5,)),
            sem((8, 2)), sem((8, 2)), sem((8, 2)), sem((8, 2)),
            sem, sem, sem,
        ],
        compiler_params=pltpu.CompilerParams(
            collective_id=0, has_side_effects=True, vmem_limit_bytes=48 * 2**20),
        cost_estimate=pl.CostEstimate(flops=flops, bytes_accessed=4 * 2**20,
                                      transcendentals=5 * 512 * 1024),
        name="gated_attention",
    )(lengths, step_index, query_rows, key_rows, value_rows, query_gain[None], key_gain[None],
      out_weight, gate_table)


def solution(mesh):
    placed = (
        P("slot", ("head", "blk"), None),
        P("slot", ("head", "blk"), None),
        P("slot", ("head", "blk"), None),
        P(),
        P(),
        P("head", ("slot", "blk")),
        P(),
        P("slot"),
        P("slot"),
    )
    return jax.shard_map(
        body,
        mesh=mesh,
        in_specs=placed,
        out_specs=P("slot", ("head", "blk"), None),
        check_vma=False,
    )
```

time: 264 us -> 107 us (0.41)
  waiting for transfers between devices: 165 us -> 0 us
  Pallas kernels: 0 us -> 97.4 us
  blocking collectives: 29.6 us -> 0 us
  matrix products: 25.7 us -> 0 us
  between operations: 14.1 us -> 1.32 us
  other arithmetic: 12.4 us -> 0 us
  local copies, waits for them, and re-layouts: 12.9 us -> 7.91 us
  starting transfers between devices: 3.67 us -> 0 us
    reduce_scatter x1 -> x0, waiting for transfers between devices: 109 us -> none  [body(): lax.psum_scatter(jnp.dot(attended, full_columns, preferred_element_type=j...]
    pallas_call x0 -> x1, Pallas kernels: none -> 97.4 us  [body(): pl.pallas_call(kernel, out_shape=jax.ShapeDtypeStruct((1, TOK, D), BF), i...]
    all_gather x3 -> x0, waiting for transfers between devices: 46.5 us -> none  [the longest x1 38.8 us: body(): lax.all_gather(out_weight, ('slot', 'blk'), axis=1, tiled=True)]
    all_to_all x2 -> x0, blocking collectives: 29.6 us -> none  [the longest x1 16.9 us: body(): lax.all_to_all(keys_normed, 'head', split_axis=1, concat_axis=0, tiled=True)]
    dot_general x5 -> x0, matrix products: 25.7 us -> none  [the longest x2 9.45 us: fold_block(): jnp.einsum('hqk,khd->hqd', weights.astype(jnp.bfloat16), v_split, preferr...]
    reduce_sum x5 -> x0, other arithmetic: 8.39 us -> none  [the longest x2 6.64 us: fold_block(): running_sum = running_sum * rescale + jnp.sum(weights, axis=2)]
    all_to_all x1 -> x0, waiting for transfers between devices: 8.16 us -> none  [body(): lax.all_to_all(queries, 'head', split_axis=1, concat_axis=0, tiled=True)]
    while x11 -> x0, local copies, waits for them, and re-layouts: 5.88 us -> none
  transfers between devices with their start and end apart: 5 -> 0, of which waited for: 4 -> 0; matrix products, arithmetic and copies ran while one was open for 12% -> 0% of each run, Pallas kernels for 0% -> 0%
where the time goes in v1:
time: 107 us
  Pallas kernels  97.4 us (91%)
  local copies, waits for them, and re-layouts  7.91 us (7%)
  between operations  1.32 us (1%)
    pallas_call x1, Pallas kernels, body(): pl.pallas_call(kernel, out_shape=jax.ShapeDtypeStruct((1, TOK, D), BF), i...  97.4 us
    unnamed x14, local copies, waits for them, and re-layouts  7.91 us

profile of v1, /device:TPU:1, one launch (start us, length us, event | category | flops | bytes accessed | tf_op | source)
XLA Modules:
  0.0 106.7 jit_solution(7717951925596616125)
XLA Ops:
  1.3 1.1 %copy.10.w_hbm = bf16[640,160]{1,0:T(8,128)(2,1)S(1)} copy(bf16[640,160]{0,1:T(8,128)(2,1)} %param.14) | data formatting | bytes 409600 | tf_op args[5]
  2.4 0.0 copy-start
  2.4 1.2 %copy-done = f32[50,5120]{1,0:T(8,128)S(1)} copy-done((f32[50,5120]{1,0:T(8,128)S(1)}, f32[50,5120]{1,0:T(8,128)}, u32[]{:S(2)}) %copy-start) | copy-done | bytes 1024024
  3.7 0.0 copy-start.1
  3.7 1.1 %copy-done.1 = bf16[1,64,5120]{2,1,0:T(8,128)(2,1)S(1)} copy-done((bf16[1,64,5120]{2,1,0:T(8,128)(2,1)S(1)}, bf16[1,64,5120]{2,1,0:T(8,128)(2,1)}, u32[]{:S(2)}) %copy-start.1) | copy-done | bytes 655384
  4.8 0.0 copy-start.2
  4.8 1.1 %copy-done.2 = bf16[1,64,5120]{2,1,0:T(8,128)(2,1)S(1)} copy-done((bf16[1,64,5120]{2,1,0:T(8,128)(2,1)S(1)}, bf16[1,64,5120]{2,1,0:T(8,128)(2,1)}, u32[]{:S(2)}) %copy-start.2) | copy-done | bytes 655384
  5.8 0.0 copy-start.3
  5.8 1.1 %copy-done.3 = bf16[1,64,5120]{2,1,0:T(8,128)(2,1)S(1)} copy-done((bf16[1,64,5120]{2,1,0:T(8,128)(2,1)S(1)}, bf16[1,64,5120]{2,1,0:T(8,128)(2,1)}, u32[]{:S(2)}) %copy-start.3) | copy-done | bytes 655384
  6.9 0.0 copy-start.4
  6.9 0.7 copy-done.4
  7.7 0.0 copy-start.5
  7.7 0.7 copy-done.5
  8.4 97.4 %gated_attention.1 = bf16[1,64,5120]{2,1,0:T(8,128)(2,1)S(1)} custom-call(s32[1]{0:T(128)S(6)} %copy.12.len_ref, s32[1]{0:T(128)S(6)} %copy.13.step_ref, bf16[1,64,5120]{2,1,0:T(8,128)(2,1)S(1)} %copy-done.1, bf16[1,64,5120]{2,1,0:T(8,128)(2,1)S(1)} %copy-done.2, bf16[1,64,5120]{2,1,0:T(8,128)(2,1)S(1)} %copy-done.3, f32[1,5120]{1,0:T(1,128)S(1)} %bitcast.2, ...), custom_call_target="tpu_custom_call" | custom-call | flops 4697620480 | bytes 4194304 | tf_op jit(solution)/shard_map/gated_attention/pallas_call | solution.py:520
  105.8 0.8 copy.14
Async XLA Ops:
  2.4 1.3 %copy-start = (f32[50,5120]{1,0:T(8,128)S(1)}, f32[50,5120]{1,0:T(8,128)}, u32[]{:S(2)}) copy-start(f32[50,5120]{1,0:T(8,128)} %gt_hbm.1) | copy-start | bytes 3072004
  3.7 1.1 %copy-start.1 = (bf16[1,64,5120]{2,1,0:T(8,128)(2,1)S(1)}, bf16[1,64,5120]{2,1,0:T(8,128)(2,1)}, u32[]{:S(2)}) copy-start(bf16[1,64,5120]{2,1,0:T(8,128)(2,1)} %q_hbm.1) | copy-start | bytes 1966084
  4.8 1.1 %copy-start.2 = (bf16[1,64,5120]{2,1,0:T(8,128)(2,1)S(1)}, bf16[1,64,5120]{2,1,0:T(8,128)(2,1)}, u32[]{:S(2)}) copy-start(bf16[1,64,5120]{2,1,0:T(8,128)(2,1)} %k_hbm.1) | copy-start | bytes 1966084
  5.8 1.1 %copy-start.3 = (bf16[1,64,5120]{2,1,0:T(8,128)(2,1)S(1)}, bf16[1,64,5120]{2,1,0:T(8,128)(2,1)}, u32[]{:S(2)}) copy-start(bf16[1,64,5120]{2,1,0:T(8,128)(2,1)} %v_hbm.1) | copy-start | bytes 1966084
  6.9 0.7 copy-start.4
  7.7 0.7 copy-start.5

commit v2 on v1

v2 whole, which is shorter than its diff:
```python
import functools
import math

import jax
import jax.numpy as jnp
from jax import lax
from jax.experimental import pallas as pl
from jax.experimental.pallas import tpu as pltpu
from jax.sharding import PartitionSpec as P

HD = 128
NEG_BIG = -1e30
EPSILON = 1e-06
MESH = pl.DeviceIdType.MESH

NX, NY, NZ, NC = 4, 4, 8, 2
TOK = 64
D = 5120
GW = 640
LOCAL_HEADS = GW // HD
KEYS = 1024
WC = 160
GC = 2 * WC
GROUPS = 8
AHEAD = 2
W_STEPS = ((1, 0), (2, 1), (3, 3), (4, 5))
NEAR_LAG = 2
LAST_LAG = 4
STEPS = 50
BF = jnp.bfloat16
F32 = jnp.float32


def al(value, unit):
    return pl.multiple_of(value, unit)


def kernel(
    len_ref, step_ref, q_hbm, k_hbm, v_hbm, qg_hbm, kg_hbm, w_hbm, gt_hbm, out_hbm,
    qg_ref, kg_ref, q_raw, k_raw, v_raw, q_nrm, kv_nrm, w_own, gate_tab,
    gate_row, qb, kvb, bias, wt,
    a_stage, at, pf, far_out, far_in, near_out, near_in, ft, gate_col, pair_out, pair_in, ob,
    ld, gs, gr, qs, qr, qos, ks, kr, fs, fr, w0s, w0r, zs, zr, yds, ydr,
    azs, azr, aos, aor, afs, afr, pos, por, pas, par, pfs, pfr, ffs, ffr, nns, nnr, pss, psr, fins, finr, fink,
):
    slot = lax.axis_index("slot")
    head = lax.axis_index("head")
    c = lax.axis_index("blk")
    x, zl = head // 2, head % 2
    y, zh = slot // 4, slot % 4
    z = zh * 2 + zl
    oc = 1 - c
    row_core = y % 2
    is_row_core = c == row_core
    y_pair = y + 1 - 2 * (y % 2)
    y_row = 3 - y

    def row_of(yy):
        differs = (c - yy % 2) * (c - yy % 2)
        return (1 - differs) * yy + differs * (3 - yy)
    my_row = row_of(y)
    pair_row = row_of(y_pair)

    def dev(dx, dy, dz, dc):
        return (dy * 4 + dz // 2, dx * 2 + dz % 2, dc)

    def rc(src, dst, send, recv, device):
        return pltpu.make_async_remote_copy(
            src_ref=src, dst_ref=dst, send_sem=send, recv_sem=recv,
            device_id=device, device_id_type=MESH,
        )

    def got(ref, sem):
        pltpu.make_async_copy(ref, ref, sem).wait()

    xp, xm = (x + 1) % NX, (x + 3) % NX
    zp, zm = (z + 1) % NZ, (z + 7) % NZ
    z_mate = zh * 2 + (1 - zl)
    z_out = (z + NZ - 1 + 2 * zl) % NZ
    other = dev(x, y, z, oc)
    pair = dev(x, y_pair, z, c)

    load_w = pltpu.make_async_copy(w_hbm, w_own, ld.at[0])
    load_k = pltpu.make_async_copy(k_hbm.at[0], k_raw, ld.at[1])
    load_q = pltpu.make_async_copy(q_hbm.at[0], q_raw, ld.at[2])
    load_g = [
        pltpu.make_async_copy(
            gt_hbm.at[:, pl.ds(al(row * 1280, 128), 1280)], gate_tab.at[i], ld.at[3 + i])
        for i, row in enumerate((my_row, pair_row))
    ]
    load_kg = pltpu.make_async_copy(kg_hbm, kg_ref, ld.at[5])
    load_qg = pltpu.make_async_copy(qg_hbm, qg_ref, ld.at[6])
    load_v = pltpu.make_async_copy(v_hbm.at[0], v_raw, ld.at[7])
    load_w.start()
    load_v.start()
    load_k.start()
    load_kg.start()
    load_qg.start()
    load_q.start()
    for cp in load_g:
        cp.start()

    barrier = pltpu.get_barrier_semaphore()
    partners = []
    for dh in range(8):
        for dc in range(2):
            if (dh, dc) != (0, 0):
                ph = (head + dh) % 8
                partners.append((slot, ph, (c + dc) % 2))
    partners.append(dev(x, y, z_out, c))
    partners.append(dev(x, y_row, z, c))
    partners.append(pair)
    partners.append(dev(x, y_pair, z, oc))
    for partner in partners:
        pl.semaphore_signal(barrier, inc=1, device_id=partner, device_id_type=MESH)
    pl.semaphore_wait(barrier, len(partners))

    def cols(ref, group):
        return ref.at[:, pl.ds(al(group * GW, 128), GW)]

    def kv_lanes(hh):
        return pl.ds(al(hh * 2 * HD, 2 * HD), 2 * HD)

    def q_lanes(hh):
        return pl.ds(al(hh * HD, HD), HD)

    def kv_place(hh):
        return kvb.at[pl.ds(al(c * 512 + head * TOK, TOK), TOK), kv_lanes(hh)]

    def kv_part(group, hh):
        return kv_nrm.at[:, pl.ds(al(group * 2 * GW + hh * 2 * HD, 2 * HD), 2 * HD)]

    def kv_half(which_c, hh):
        return kvb.at[pl.ds(al(which_c * 512, 512), 512), kv_lanes(hh)]

    def kv_pass(hh):
        ref = kv_half(c, hh)
        return rc(ref, ref, fs.at[hh], fr.at[hh], other)

    q_core = x // 2
    q_stays = c == q_core
    q_row = zl * 256 + (x % 2) * 128 + c * TOK

    def q_place(hh):
        return qb.at[pl.ds(al(q_row, TOK), TOK), q_lanes(hh)]

    def q_part(group, hh):
        return q_nrm.at[:, pl.ds(al(group * GW + hh * HD, HD), HD)]

    def q_copy(group, hh, send):
        return rc(q_part(group, hh), q_place(hh), send, qr.at[hh], (slot, group, q_core))

    def send_head(hh):
        pltpu.make_async_copy(kv_part(head, hh), kv_place(hh), kr.at[hh]).start()

        @pl.when(q_stays)
        def _():
            pltpu.make_async_copy(q_part(head, hh), q_place(hh), qr.at[hh]).start()

        @pl.when(jnp.logical_not(q_stays))
        def _():
            q_copy(head, hh, qos.at[hh]).start()

        def one(t, carry):
            group = (head + t) % 8
            rc(kv_part(group, hh), kv_place(hh), ks.at[hh], kr.at[hh], (slot, group, c)).start()
            q_copy(group, hh, qs.at[hh]).start()
            return carry
        lax.fori_loop(1, 8, one, 0)

    def head_sent(hh):
        got(kvb.at[pl.ds(0, 7 * TOK), kv_lanes(hh)], ks.at[hh])
        got(qb.at[pl.ds(0, 7 * TOK), q_lanes(hh)], qs.at[hh])

    def head_here(hh):
        got(kv_half(c, hh), kr.at[hh])
        kv_pass(hh).start()
        got(qb.at[:, q_lanes(hh)], qr.at[hh])
        got(kv_half(oc, hh), fr.at[hh])

    def piece(zsrc, half=None):
        row = (zsrc // 2) * GC
        size = GC
        if half is not None:
            row = row + half * WC
            size = WC
        return wt.at[pl.ds(al(row, 32), size), pl.ds(al((zsrc % 2) * GW, 128), GW)]

    load_w.wait()

    @pl.when(is_row_core)
    def _():
        pltpu.make_async_copy(w_own, piece(z, c), w0r.at[c]).start()

    @pl.when(jnp.logical_not(is_row_core))
    def _():
        rc(w_own, piece(z, c), w0s, w0r.at[c], other).start()

    def row_send(zsrc, j):
        return rc(piece(zsrc), piece(zsrc), yds.at[j], ydr.at[j], dev(x, y_row, z, c))

    def z_send(d, k):
        zsrc = (z + NZ - (k - 1)) % NZ if d == 0 else (z + k - 1) % NZ
        half = None if k < 4 else d
        return rc(piece(zsrc, half), piece(zsrc, half), zs.at[d, k - 1], zr.at[d, k - 1],
                  dev(x, y, zp if d == 0 else zm, c))

    def z_from(d, k):
        return (z + NZ - k) % NZ if d == 0 else (z + k) % NZ

    def z_index(d, k):
        ahead = zl if d == 0 else 1 - zl
        if k == 1:
            return 2 - ahead
        if k == 2:
            return 3 + ahead
        return 6 - ahead

    def z_first():
        @pl.when(is_row_core)
        def _():
            got(piece(z, 0), w0r.at[0])
            got(piece(z, 1), w0r.at[1])
            for d in range(2):
                z_send(d, 1).start()
            row_send(z, 0).start()

    def z_service(k):
        @pl.when(is_row_core)
        def _():
            for d in range(2):
                zsrc = z_from(d, k)
                got(piece(zsrc), zr.at[d, k - 1])
                z_send(d, k + 1).start()
                row_send(zsrc, z_index(d, k)).start()

    def z_last():
        @pl.when(is_row_core)
        def _():
            zsrc = (z + 4) % NZ
            for d in range(2):
                got(piece(zsrc, d), zr.at[d, 3])
            row_send(zsrc, 7).start()

    sgn = 1 - 2 * zl
    DELTA = (0, 1, -1, -2, 2, 3, -3, 4)

    def z_of(j):
        return (z + NZ + sgn * DELTA[j]) % NZ

    def row_wait(p):
        @pl.when(jnp.logical_not(is_row_core))
        def _():
            for j in (2 * p, 2 * p + 1):
                got(piece(z_of(j)), ydr.at[j])

    def normed(raw, gain_ref, here):
        vals = raw[here, :].astype(F32)
        mean_square = jnp.mean(vals * vals, axis=-1, keepdims=True)
        return (vals * lax.rsqrt(mean_square + EPSILON) * gain_ref[...]).astype(BF)

    def kv_rows(i, carry):
        here = pl.ds(al(i * 16, 16), 16)
        out = normed(k_raw, kg_ref, here)
        for hh in range(D // HD):
            src = slice(hh * HD, hh * HD + HD)
            kv_nrm[here, hh * 2 * HD:hh * 2 * HD + HD] = out[:, src]
            kv_nrm[here, hh * 2 * HD + HD:hh * 2 * HD + 2 * HD] = v_raw[here, src]
        return carry

    def q_rows(i, carry):
        here = pl.ds(al(i * 16, 16), 16)
        q_nrm[here, :] = normed(q_raw, qg_ref, here)
        return carry

    load_k.wait()
    load_kg.wait()
    load_v.wait()
    lax.fori_loop(0, TOK // 16, kv_rows, 0)
    load_q.wait()
    load_qg.wait()
    lax.fori_loop(0, TOK // 16, q_rows, 0)
    send_head(0)
    z_first()
    for hh in range(1, AHEAD):
        send_head(hh)

    def mask_rows(i, carry):
        row = lax.broadcasted_iota(jnp.int32, (TOK, 128), 0)
        pos = (i % 8) * 128 + (i // 8) * TOK + row
        bias[pl.ds(al(i * TOK, TOK), TOK), :] = jnp.where(pos < len_ref[0], 0.0, NEG_BIG)
        return carry
    lax.fori_loop(0, KEYS // TOK, mask_rows, 0)

    step_rows = lax.broadcasted_iota(jnp.int32, (STEPS, 1280), 0)
    for i in range(2):
        load_g[i].wait()
        gate_row[i] = jnp.sum(
            jnp.where(step_rows == step_ref[0], gate_tab[i], 0.0), axis=0, keepdims=True)
    gate_copy = rc(gate_row.at[1], gate_row.at[2], gs, gr, pair)
    gate_copy.start()

    scale = math.log2(math.e) / math.sqrt(HD)
    mine = pl.ds(al(c * 256, 128), 256)
    theirs = pl.ds(al(oc * 256, 128), 256)
    pair_mine = pl.ds(al(512 + c * 256, 128), 256)
    pair_theirs = pl.ds(al(512 + oc * 256, 128), 256)

    def feats(which_zl, hh):
        return pl.ds(al(which_zl * GW + hh * HD, HD), HD)

    def attend(hh, zq):
        lanes = q_lanes(hh)
        keys = kvb[:, pl.ds(al(hh * 2 * HD, HD), HD)]
        values = kvb[:, pl.ds(al(hh * 2 * HD + HD, HD), HD)]
        queries = qb[pl.ds(al(zq * 256, 256), 256), lanes]
        scores = lax.dot_general(keys, queries, (((1,), (1,)), ((), ())),
                                 preferred_element_type=F32)
        scores = scores * scale + jnp.concatenate([bias[...], bias[...]], axis=1)
        top = jnp.max(scores, axis=0, keepdims=True)
        weights = jnp.exp2(scores - top)
        total = jnp.sum(weights, axis=0, keepdims=True)
        mixed = lax.dot_general(values, weights.astype(BF), (((0,), (0,)), ((), ())),
                                preferred_element_type=F32)
        return (mixed / total).astype(BF)

    def away_copy(hh):
        return rc(a_stage.at[hh], at.at[feats(zl, hh), mine], azs.at[hh], azr.at[hh],
                  dev(x, y, z_mate, c))

    def home_copy(hh):
        ref = at.at[feats(zl, hh), mine]
        return rc(ref, ref, aos.at[hh], aor.at[hh], other)

    def pass_copy(hh):
        ref = at.at[feats(1 - zl, hh), mine]
        return rc(ref, ref, afs.at[hh], afr.at[hh], other)

    def pair_home_copy(hh):
        return rc(at.at[feats(zl, hh), mine], at.at[feats(zl, hh), pair_mine],
                  pos.at[hh], por.at[hh], pair)

    def pair_pass_copy(hh):
        return rc(at.at[feats(1 - zl, hh), mine], at.at[feats(1 - zl, hh), pair_mine],
                  pas.at[hh], par.at[hh], pair)

    def pair_share_copy(hh, which):
        ref = at.at[feats(which, hh), pair_mine]
        return rc(ref, ref, pfs.at[hh, which], pfr.at[hh, which], other)

    def one_head(hh):
        a_stage[hh] = attend(hh, 1 - zl)
        away_copy(hh).start()
        at[feats(zl, hh), mine] = attend(hh, zl)
        pair_home_copy(hh).start()
        home_copy(hh).start()

    def pass_on(hh, carry):
        got(at.at[feats(1 - zl, hh), mine], azr.at[hh])
        pair_pass_copy(hh).start()
        pass_copy(hh).start()
        return carry

    def w_steps(hh):
        for k, when in W_STEPS:
            @pl.when(hh == when)
            def _(k=k):
                z_service(k) if k < 4 else z_last()

    def heads(hh, carry):
        w_steps(hh)

        @pl.when(hh + AHEAD < LOCAL_HEADS)
        def _():
            head_sent(hh)
            send_head(hh + AHEAD)
        head_here(hh)
        one_head(hh)

        @pl.when(hh > 0)
        def _():
            pass_on(hh - 1, 0)
        return carry
    lax.fori_loop(0, LOCAL_HEADS, heads, 0)
    w_steps(LOCAL_HEADS)
    pass_on(LOCAL_HEADS - 1, 0)

    def attended_wait(hh, carry):
        got(at.at[feats(zl, hh), theirs], aor.at[hh])
        got(at.at[feats(1 - zl, hh), theirs], afr.at[hh])
        return carry
    lax.fori_loop(0, LOCAL_HEADS, attended_wait, 0)

    def pair_share(hh, carry):
        got(at.at[feats(zl, hh), pair_mine], por.at[hh])
        pair_share_copy(hh, zl).start()
        got(at.at[feats(1 - zl, hh), pair_mine], par.at[hh])
        pair_share_copy(hh, 1 - zl).start()
        return carry

    def pair_wait(hh, carry):
        for which in range(2):
            got(at.at[feats(which, hh), pair_theirs], pfr.at[hh, which])
        return carry

    def past(i, k):
        return jnp.where(i >= k, 1, 0)

    def slot_of(i):
        return past(i, 2) - past(i, 4) + past(i, 5) - past(i, 7)

    def group_p(i):
        return past(i, 1) - past(i, 2) + past(i, 3) + past(i, 4) + past(i, 6)

    def group_of(i):
        return zh_of(group_p(i))

    def zh_of(p):
        is1 = (p % 2) * (1 - p // 2)
        is2 = (1 - p % 2) * (p // 2)
        is3 = (p % 2) * (p // 2)
        return (zh + 4 - sgn * is1 + sgn * is2 + 2 * is3) % 4

    def lane_block(xx):
        return pl.ds(al(xx * 128, 128), 128)

    def far_copies(i):
        yield rc(far_out.at[i, pl.ds(0, WC), :], far_in.at[i, 0], ffs.at[i, 0], ffr.at[i, 0],
                 dev(xp, y, z, c))
        yield rc(far_out.at[i, pl.ds(WC, WC), :], far_in.at[i, 1], ffs.at[i, 1], ffr.at[i, 1],
                 dev(xm, y, z, c))

    def near_copies(i):
        yield rc(near_out.at[i, 0], near_in.at[i, 0], nns.at[i, 0], nnr.at[i, 0], dev(xp, y, z, c))
        yield rc(near_out.at[i, 1], near_in.at[i, 1], nns.at[i, 1], nnr.at[i, 1], dev(xm, y, z, c))

    def stage_a(i):
        rows = pl.ds(al(group_of(i) * GC, 32), GC)
        lanes = pl.ds(al(slot_of(i) * 512, 128), 512)
        pf[i] = jnp.dot(wt[rows, :], at[:, lanes], preferred_element_type=F32)
        far_out[i] = pf[i, :, lane_block((x + 2) % NX)].astype(BF)
        for cp in far_copies(i):
            cp.start()

    def stage_b(i):
        for d in range(2):
            got(far_in.at[i, d], ffr.at[i, d])
        up = lane_block(xp)
        down = lane_block(xm)
        lo, hi = pl.ds(0, WC), pl.ds(WC, WC)
        near_out[i, 0, lo, :] = (pf[i, lo, up] + far_in[i, 0].astype(F32)).astype(BF)
        near_out[i, 0, hi, :] = pf[i, hi, up].astype(BF)
        near_out[i, 1, lo, :] = pf[i, lo, down].astype(BF)
        near_out[i, 1, hi, :] = (pf[i, hi, down] + far_in[i, 1].astype(F32)).astype(BF)
        for cp in near_copies(i):
            cp.start()

    def stage_c(i):
        for d in range(2):
            got(near_in.at[i, d], nnr.at[i, d])
        rows = pl.ds(al(group_of(i) * GC, 32), GC)
        total = (pf[i, :, lane_block(x)] + near_in[i, 0].astype(F32)
                 + near_in[i, 1].astype(F32))
        whose = slot_of(i)

        @pl.when(whose == 0)
        def _():
            ft[rows, :] = total

        @pl.when(whose == 1)
        def _():
            pair_out[rows, :] = (total * gate_col[rows, :]).astype(BF)
            pair_sum(group_p(i)).start()

    def pair_sum(p):
        rows = pl.ds(al(zh_of(p) * GC, 32), GC)
        return rc(pair_out.at[rows, :], pair_in.at[rows, :], pss.at[p], psr.at[p], pair)

    def step(i, carry):
        for p, when in enumerate((0, 1, 4, 6)):
            @pl.when(i == when)
            def _(p=p):
                row_wait(p)

        @pl.when(i == 1)
        def _():
            lax.fori_loop(0, LOCAL_HEADS, pair_share, 0)

        @pl.when(i == 2)
        def _():
            lax.fori_loop(0, LOCAL_HEADS, pair_wait, 0)

        @pl.when(i < GROUPS)
        def _():
            stage_a(i)

        @pl.when(jnp.logical_and(i >= NEAR_LAG, i < GROUPS + NEAR_LAG))
        def _():
            stage_b(i - NEAR_LAG)

        @pl.when(i >= LAST_LAG)
        def _():
            stage_c(i - LAST_LAG)
        return carry
    def tokens(which, cc):
        return ob.at[which, pl.ds(al(cc * TOK, TOK), TOK), :]

    def out_cols(row):
        return out_hbm.at[0, :, pl.ds(al(row * 1280, 128), 1280)]

    keep = [pltpu.make_async_copy(tokens(i, c), out_cols(row), fink.at[i])
            for i, row in enumerate((my_row, pair_row))]
    give = [rc(tokens(i, oc), out_cols(row), fins.at[i], finr.at[i], other)
            for i, row in enumerate((my_row, pair_row))]
    got(gate_row.at[2], gr)
    gate_col[...] = jnp.broadcast_to(gate_row[2], (128, 1280)).T
    lax.fori_loop(0, GROUPS + LAST_LAG - 1, step, 0)
    stage_c(GROUPS - 1)
    for b in range(10):
        here = slice(b * 128, b * 128 + 128)
        ob[0, :, here] = (ft[here, :].T * gate_row[0, :, here]).astype(BF)
    keep[0].start()
    give[0].start()
    for p in range(4):
        got(pair_in.at[pl.ds(al(zh_of(p) * GC, 32), GC), :], psr.at[p])
    for b in range(10):
        here = slice(b * 128, b * 128 + 128)
        ob[1, :, here] = pair_in[here, :].T
    keep[1].start()
    give[1].start()

    for hh in range(LOCAL_HEADS - AHEAD, LOCAL_HEADS):
        head_sent(hh)

    def head_passed(hh, carry):
        @pl.when(jnp.logical_not(q_stays))
        def _():
            q_copy(head, hh, qos.at[hh]).wait_send()
        kv_pass(hh).wait_send()
        return carry
    lax.fori_loop(0, LOCAL_HEADS, head_passed, 0)

    @pl.when(jnp.logical_not(is_row_core))
    def _():
        rc(w_own, piece(z, c), w0s, w0r.at[c], other).wait_send()

    @pl.when(is_row_core)
    def _():
        for d in range(2):
            for k in range(1, 5):
                z_send(d, k).wait_send()
        row_send(z, 0).wait_send()
        for k in range(1, 4):
            for d in range(2):
                row_send(z_from(d, k), z_index(d, k)).wait_send()
        row_send((z + 4) % NZ, 7).wait_send()

    def heads_sent(hh, carry):
        away_copy(hh).wait_send()
        home_copy(hh).wait_send()
        pass_copy(hh).wait_send()
        pair_home_copy(hh).wait_send()
        pair_pass_copy(hh).wait_send()
        for which in range(2):
            pair_share_copy(hh, which).wait_send()
        return carry
    lax.fori_loop(0, LOCAL_HEADS, heads_sent, 0)

    def sums_sent(i, carry):
        for cp in far_copies(i):
            cp.wait_send()
        for cp in near_copies(i):
            cp.wait_send()
        return carry
    lax.fori_loop(0, GROUPS, sums_sent, 0)
    gate_copy.wait_send()
    for p in range(4):
        pair_sum(p).wait_send()
    for i, yy in enumerate((y, y_pair)):
        keep[i].wait()
        give[i].wait_send()
        differs = (oc - yy % 2) * (oc - yy % 2)
        got(out_cols((1 - differs) * yy + differs * (3 - yy)), finr.at[i])


def body(query_rows, key_rows, value_rows, query_gain, key_gain, out_weight, gate_table, lengths,
         step_index):
    smem = pl.BlockSpec(memory_space=pltpu.SMEM)
    hbm = pl.BlockSpec(memory_space=pl.ANY)
    sem = pltpu.SemaphoreType.DMA
    flops = 2 * (2 * 5 * 512 * 1024 * 128 + 512 * 1280 * 2560)
    return pl.pallas_call(
        kernel,
        out_shape=jax.ShapeDtypeStruct((1, TOK, D), BF),
        in_specs=[smem, smem] + [hbm] * 7,
        out_specs=hbm,
        scratch_shapes=[
            pltpu.VMEM((1, D), F32),
            pltpu.VMEM((1, D), F32),
            pltpu.VMEM((TOK, D), BF),
            pltpu.VMEM((TOK, D), BF),
            pltpu.VMEM((TOK, D), BF),
            pltpu.VMEM((TOK, D), BF),
            pltpu.VMEM((TOK, 2 * D), BF),
            pltpu.VMEM((WC, GW), BF),
            pltpu.VMEM((2, STEPS, 1280), F32),
            pltpu.VMEM((3, 1, 1280), F32),
            pltpu.VMEM((512, GW), BF),
            pltpu.VMEM((KEYS, 2 * GW), BF),
            pltpu.VMEM((KEYS, 128), F32),
            pltpu.VMEM((1280, 2 * GW), BF),
            pltpu.VMEM((LOCAL_HEADS, HD, 256), BF),
            pltpu.VMEM((2 * GW, 1024), BF),
            pltpu.VMEM((GROUPS, GC, 512), F32),
            pltpu.VMEM((GROUPS, GC, 128), BF),
            pltpu.VMEM((GROUPS, 2, WC, 128), BF),
            pltpu.VMEM((GROUPS, 2, GC, 128), BF),
            pltpu.VMEM((GROUPS, 2, GC, 128), BF),
            pltpu.VMEM((1280, 128), F32),
            pltpu.VMEM((1280, 128), F32),
            pltpu.VMEM((1280, 128), BF),
            pltpu.VMEM((1280, 128), BF),
            pltpu.VMEM((2, 128, 1280), BF),
            sem((8,)),
            sem, sem,
            sem((5,)), sem((5,)), sem((5,)), sem((5,)), sem((5,)),
            sem((5,)), sem((5,)),
            sem, sem((2,)),
            sem((2, 4)), sem((2, 4)),
            sem((8,)), sem((8,)),
            sem((5,)), sem((5,)), sem((5,)), sem((5,)), sem((5,)), sem((5,)),
            sem((5,)), sem((5,)), sem((5,)), sem((5,)), sem((5, 2)), sem((5, 2)),
            sem((8, 2)), sem((8, 2)), sem((8, 2)), sem((8, 2)),
            sem((4,)), sem((4,)),
            sem((2,)), sem((2,)), sem((2,)),
        ],
        compiler_params=pltpu.CompilerParams(
            collective_id=0, has_side_effects=True, vmem_limit_bytes=60 * 2**20),
        cost_estimate=pl.CostEstimate(flops=flops, bytes_accessed=4 * 2**20,
                                      transcendentals=5 * 512 * 1024),
        name="gated_attention",
    )(lengths, step_index, query_rows, key_rows, value_rows, query_gain[None], key_gain[None],
      out_weight.T, gate_table)


def solution(mesh):
    placed = (
        P("slot", ("head", "blk"), None),
        P("slot", ("head", "blk"), None),
        P("slot", ("head", "blk"), None),
        P(),
        P(),
        P("head", ("slot", "blk")),
        P(),
        P("slot"),
        P("slot"),
    )
    return jax.shard_map(
        body,
        mesh=mesh,
        in_specs=placed,
        out_specs=P("slot", ("head", "blk"), None),
        check_vma=False,
    )
```

time: 107 us -> 92 us (0.86)
  Pallas kernels: 97.4 us -> 88.6 us
  local copies, waits for them, and re-layouts: 7.91 us -> 1.97 us
    pallas_call x1, Pallas kernels: 97.4 us -> 88.6 us  [body(): pl.pallas_call(kernel, out_shape=jax.ShapeDtypeStruct((1, TOK, D), BF), i...]
    unnamed x14 -> x1, local copies, waits for them, and re-layouts: 7.91 us -> 1.97 us
where the time goes in v2:
time: 92 us; the launch traced here: 91.9 us
  Pallas kernels  88.6 us (96%)
  local copies, waits for them, and re-layouts  1.97 us (2%)
  between operations  1.3 us (1%)
    pallas_call x1, Pallas kernels, body(): pl.pallas_call(kernel, out_shape=jax.ShapeDtypeStruct((1, TOK, D), BF), i...  88.6 us
    unnamed x1, local copies, waits for them, and re-layouts  1.97 us

profile of v2, /device:TPU:1, one launch (start us, length us, event | category | flops | bytes accessed | tf_op | source)
XLA Modules:
  0.0 91.9 jit_solution(5784289566396973232)
XLA Ops:
  1.3 88.6 %gated_attention.1 = bf16[1,64,5120]{2,1,0:T(8,128)(2,1)} custom-call(s32[1]{0:T(128)S(6)} %copy.11.len_ref, s32[1]{0:T(128)S(6)} %copy.12.step_ref, bf16[1,64,5120]{2,1,0:T(8,128)(2,1)} %q_hbm.1, bf16[1,64,5120]{2,1,0:T(8,128)(2,1)} %k_hbm.1, bf16[1,64,5120]{2,1,0:T(8,128)(2,1)} %v_hbm.1, f32[1,5120]{1,0:T(1,128)} %bitcast.4, f32[1,5120]{1,0:T(1,128)} %bitcast.5, ...), custom_call_target="tpu_custom_call" | custom-call | flops 4697620480 | bytes 4194304 | tf_op jit(solution)/shard_map/gated_attention/pallas_call | solution.py:592
  89.9 2.0 %copy.13 = bf16[1,64,5120]{2,1,0:T(8,128)(2,1)} copy(bf16[1,64,5120]{2,1,0:T(8,128)(2,1)} %gated_attention.1) | data formatting | bytes 1310720

commit v3 on v2

--- a/solution.py
+++ b/solution.py
@@ -23,7 +23,7 @@
 GC = 2 * WC
 GROUPS = 8
 AHEAD = 2
-W_STEPS = ((1, 0), (2, 1), (3, 3), (4, 5))
+W_STEPS = ((-1, 1), (1, 1), (-2, 3), (2, 3), (-3, 5), (3, 5), (-4, 12))
 NEAR_LAG = 2
 LAST_LAG = 4
 STEPS = 50
@@ -201,8 +201,7 @@
 
     def z_send(d, k):
         zsrc = (z + NZ - (k - 1)) % NZ if d == 0 else (z + k - 1) % NZ
-        half = None if k < 4 else d
-        return rc(piece(zsrc, half), piece(zsrc, half), zs.at[d, k - 1], zr.at[d, k - 1],
+        return rc(piece(zsrc), piece(zsrc), zs.at[d, k - 1], zr.at[d, k - 1],
                   dev(x, y, zp if d == 0 else zm, c))
 
     def z_from(d, k):
@@ -225,21 +224,30 @@
                 z_send(d, 1).start()
             row_send(z, 0).start()
 
-    def z_service(k):
+    def z_take(k):
         @pl.when(is_row_core)
         def _():
             for d in range(2):
                 zsrc = z_from(d, k)
                 got(piece(zsrc), zr.at[d, k - 1])
-                z_send(d, k + 1).start()
                 row_send(zsrc, z_index(d, k)).start()
+
+    def z_on(k):
+        @pl.when(is_row_core)
+        def _():
+            for d in range(2):
+                if k < 3:
+                    z_send(d, k + 1).start()
+                else:
+                    @pl.when(d == 1 - zl)
+                    def _(d=d):
+                        z_send(d, 4).start()
 
     def z_last():
         @pl.when(is_row_core)
         def _():
             zsrc = (z + 4) % NZ
-            for d in range(2):
-                got(piece(zsrc, d), zr.at[d, 3])
+            got(piece(zsrc), zr.at[zl, 3])
             row_send(zsrc, 7).start()
 
     sgn = 1 - 2 * zl
@@ -299,6 +307,9 @@
             jnp.where(step_rows == step_ref[0], gate_tab[i], 0.0), axis=0, keepdims=True)
     gate_copy = rc(gate_row.at[1], gate_row.at[2], gs, gr, pair)
     gate_copy.start()
+
+    got(gate_row.at[2], gr)
+    gate_col[...] = jnp.broadcast_to(gate_row[2], (128, 1280)).T
 
     scale = math.log2(math.e) / math.sqrt(HD)
     mine = pl.ds(al(c * 256, 128), 256)
@@ -361,11 +372,15 @@
         pass_copy(hh).start()
         return carry
 
-    def w_steps(hh):
+    def w_steps(hh, first=0):
         for k, when in W_STEPS:
-            @pl.when(hh == when)
-            def _(k=k):
-                z_service(k) if k < 4 else z_last()
+            if first <= when < first + 10:
+                @pl.when(hh == when - first)
+                def _(k=k):
+                    if k == -4:
+                        z_last()
+                    else:
+                        z_take(-k) if k < 0 else z_on(k)
 
     def heads(hh, carry):
         w_steps(hh)
@@ -476,6 +491,55 @@
         rows = pl.ds(al(zh_of(p) * GC, 32), GC)
         return rc(pair_out.at[rows, :], pair_in.at[rows, :], pss.at[p], psr.at[p], pair)
 
+    def inputs_sent():
+        for hh in range(LOCAL_HEADS - AHEAD, LOCAL_HEADS):
+            head_sent(hh)
+
+        def head_passed(hh, carry):
+            @pl.when(jnp.logical_not(q_stays))
+            def _():
+                q_copy(head, hh, qos.at[hh]).wait_send()
+            kv_pass(hh).wait_send()
+            return carry
+        lax.fori_loop(0, LOCAL_HEADS, head_passed, 0)
+
+        def heads_sent(hh, carry):
+            away_copy(hh).wait_send()
+            home_copy(hh).wait_send()
+            pass_copy(hh).wait_send()
+            pair_home_copy(hh).wait_send()
+            pair_pass_copy(hh).wait_send()
+            for which in range(2):
+                pair_share_copy(hh, which).wait_send()
+            return carry
+        lax.fori_loop(0, LOCAL_HEADS, heads_sent, 0)
+
+    def weights_sent():
+        @pl.when(jnp.logical_not(is_row_core))
+        def _():
+            rc(w_own, piece(z, c), w0s, w0r.at[c], other).wait_send()
+
+        @pl.when(is_row_core)
+        def _():
+            for d in range(2):
+                for k in range(1, 4):
+                    z_send(d, k).wait_send()
+
+                @pl.when(d == 1 - zl)
+                def _(d=d):
+                    z_send(d, 4).wait_send()
+            row_send(z, 0).wait_send()
+            for k in range(1, 4):
+                for d in range(2):
+                    row_send(z_from(d, k), z_index(d, k)).wait_send()
+            row_send((z + 4) % NZ, 7).wait_send()
+
+    def sums_sent(i):
+        for cp in far_copies(i):
+            cp.wait_send()
+        for cp in near_copies(i):
+            cp.wait_send()
+
     def step(i, carry):
         for p, when in enumerate((0, 1, 4, 6)):
             @pl.when(i == when)
@@ -501,6 +565,19 @@
         @pl.when(i >= LAST_LAG)
         def _():
             stage_c(i - LAST_LAG)
+        w_steps(i, 10)
+
+        @pl.when(i == 5)
+        def _():
+            inputs_sent()
+
+        @pl.when(i == GROUPS + LAST_LAG - 2)
+        def _():
+            weights_sent()
+
+        @pl.when(i >= LAST_LAG + 1)
+        def _():
+            sums_sent(i - LAST_LAG - 1)
         return carry
     def tokens(which, cc):
         return ob.at[which, pl.ds(al(cc * TOK, TOK), TOK), :]
@@ -512,8 +589,6 @@
             for i, row in enumerate((my_row, pair_row))]
     give = [rc(tokens(i, oc), out_cols(row), fins.at[i], finr.at[i], other)
             for i, row in enumerate((my_row, pair_row))]
-    got(gate_row.at[2], gr)
-    gate_col[...] = jnp.broadcast_to(gate_row[2], (128, 1280)).T
     lax.fori_loop(0, GROUPS + LAST_LAG - 1, step, 0)
     stage_c(GROUPS - 1)
     for b in range(10):
@@ -529,50 +604,8 @@
     keep[1].start()
     give[1].start()
 
-    for hh in range(LOCAL_HEADS - AHEAD, LOCAL_HEADS):
-        head_sent(hh)
-
-    def head_passed(hh, carry):
-        @pl.when(jnp.logical_not(q_stays))
-        def _():
-            q_copy(head, hh, qos.at[hh]).wait_send()
-        kv_pass(hh).wait_send()
-        return carry
-    lax.fori_loop(0, LOCAL_HEADS, head_passed, 0)
-
-    @pl.when(jnp.logical_not(is_row_core))
-    def _():
-        rc(w_own, piece(z, c), w0s, w0r.at[c], other).wait_send()
-
-    @pl.when(is_row_core)
-    def _():
-        for d in range(2):
-            for k in range(1, 5):
-                z_send(d, k).wait_send()
-        row_send(z, 0).wait_send()
-        for k in range(1, 4):
-            for d in range(2):
-                row_send(z_from(d, k), z_index(d, k)).wait_send()
-        row_send((z + 4) % NZ, 7).wait_send()
-
-    def heads_sent(hh, carry):
-        away_copy(hh).wait_send()
-        home_copy(hh).wait_send()
-        pass_copy(hh).wait_send()
-        pair_home_copy(hh).wait_send()
-        pair_pass_copy(hh).wait_send()
-        for which in range(2):
-            pair_share_copy(hh, which).wait_send()
-        return carry
-    lax.fori_loop(0, LOCAL_HEADS, heads_sent, 0)
-
-    def sums_sent(i, carry):
-        for cp in far_copies(i):
-            cp.wait_send()
-        for cp in near_copies(i):
-            cp.wait_send()
-        return carry
-    lax.fori_loop(0, GROUPS, sums_sent, 0)
+    for i in range(GROUPS - 2, GROUPS):
+        sums_sent(i)
     gate_copy.wait_send()
     for p in range(4):
         pair_sum(p).wait_send()

time: 92 us -> 88.9 us (0.966)
  Pallas kernels: 88.6 us -> 85.5 us
    pallas_call x1, Pallas kernels: 88.6 us -> 85.5 us  [body(): pl.pallas_call(kernel, out_shape=jax.ShapeDtypeStruct((1, TOK, D), BF), i...]
where the time goes in v3:
time: 88.9 us; the launch traced here: 88.8 us
  Pallas kernels  85.5 us (96%)
  local copies, waits for them, and re-layouts  1.97 us (2%)
  between operations  1.3 us (1%)
    pallas_call x1, Pallas kernels, body(): pl.pallas_call(kernel, out_shape=jax.ShapeDtypeStruct((1, TOK, D), BF), i...  85.5 us
    unnamed x1, local copies, waits for them, and re-layouts  1.97 us

profile of v3, /device:TPU:1, one launch (start us, length us, event | category | flops | bytes accessed | tf_op | source)
XLA Modules:
  0.0 88.8 jit_solution(2225920531093154679)
XLA Ops:
  1.3 85.5 %gated_attention.1 = bf16[1,64,5120]{2,1,0:T(8,128)(2,1)} custom-call(s32[1]{0:T(128)S(6)} %copy.11.len_ref, s32[1]{0:T(128)S(6)} %copy.12.step_ref, bf16[1,64,5120]{2,1,0:T(8,128)(2,1)} %q_hbm.1, bf16[1,64,5120]{2,1,0:T(8,128)(2,1)} %k_hbm.1, bf16[1,64,5120]{2,1,0:T(8,128)(2,1)} %v_hbm.1, f32[1,5120]{1,0:T(1,128)} %bitcast.4, f32[1,5120]{1,0:T(1,128)} %bitcast.5, ...), custom_call_target="tpu_custom_call" | custom-call | flops 4697620480 | bytes 4194304 | tf_op jit(solution)/shard_map/gated_attention/pallas_call | solution.py:625
  86.8 2.0 %copy.13 = bf16[1,64,5120]{2,1,0:T(8,128)(2,1)} copy(bf16[1,64,5120]{2,1,0:T(8,128)(2,1)} %gated_attention.1) | data formatting | bytes 1310720

commit v4 on v3

--- a/solution.py
+++ b/solution.py
@@ -23,7 +23,7 @@
 GC = 2 * WC
 GROUPS = 8
 AHEAD = 2
-W_STEPS = ((-1, 1), (1, 1), (-2, 3), (2, 3), (-3, 5), (3, 5), (-4, 12))
+W_STEPS = ((-1, 1), (1, 1), (-2, 3), (2, 3), (-3, 5), (3, 5), (-4, 13))
 NEAR_LAG = 2
 LAST_LAG = 4
 STEPS = 50
@@ -113,7 +113,6 @@
     partners.append(dev(x, y_pair, z, oc))
     for partner in partners:
         pl.semaphore_signal(barrier, inc=1, device_id=partner, device_id_type=MESH)
-    pl.semaphore_wait(barrier, len(partners))
 
     def cols(ref, group):
         return ref.at[:, pl.ds(al(group * GW, 128), GW)]
@@ -186,16 +185,6 @@
             size = WC
         return wt.at[pl.ds(al(row, 32), size), pl.ds(al((zsrc % 2) * GW, 128), GW)]
 
-    load_w.wait()
-
-    @pl.when(is_row_core)
-    def _():
-        pltpu.make_async_copy(w_own, piece(z, c), w0r.at[c]).start()
-
-    @pl.when(jnp.logical_not(is_row_core))
-    def _():
-        rc(w_own, piece(z, c), w0s, w0r.at[c], other).start()
-
     def row_send(zsrc, j):
         return rc(piece(zsrc), piece(zsrc), yds.at[j], ydr.at[j], dev(x, y_row, z, c))
 
@@ -288,10 +277,21 @@
     load_q.wait()
     load_qg.wait()
     lax.fori_loop(0, TOK // 16, q_rows, 0)
-    send_head(0)
+
+    pl.semaphore_wait(barrier, len(partners))
+    load_w.wait()
+
+    @pl.when(is_row_core)
+    def _():
+        pltpu.make_async_copy(w_own, piece(z, c), w0r.at[c]).start()
+
+    @pl.when(jnp.logical_not(is_row_core))
+    def _():
+        rc(w_own, piece(z, c), w0s, w0r.at[c], other).start()
+
+    for hh in range(AHEAD):
+        send_head(hh)
     z_first()
-    for hh in range(1, AHEAD):
-        send_head(hh)
 
     def mask_rows(i, carry):
         row = lax.broadcasted_iota(jnp.int32, (TOK, 128), 0)
@@ -383,14 +383,13 @@
                         z_take(-k) if k < 0 else z_on(k)
 
     def heads(hh, carry):
-        w_steps(hh)
-
         @pl.when(hh + AHEAD < LOCAL_HEADS)
         def _():
             head_sent(hh)
             send_head(hh + AHEAD)
         head_here(hh)
         one_head(hh)
+        w_steps(hh)
 
         @pl.when(hh > 0)
         def _():

time: 88.9 us -> 87.8 us (0.988)
  Pallas kernels: 85.5 us -> 84.3 us
    pallas_call x1, Pallas kernels: 85.5 us -> 84.3 us  [body(): pl.pallas_call(kernel, out_shape=jax.ShapeDtypeStruct((1, TOK, D), BF), i...]
where the time goes in v4:
time: 87.8 us; the launch traced here: 87.6 us
  Pallas kernels  84.3 us (96%)
  local copies, waits for them, and re-layouts  1.97 us (2%)
  between operations  1.3 us (1%)
    pallas_call x1, Pallas kernels, body(): pl.pallas_call(kernel, out_shape=jax.ShapeDtypeStruct((1, TOK, D), BF), i...  84.3 us
    unnamed x1, local copies, waits for them, and re-layouts  1.97 us

profile of v4, /device:TPU:1, one launch (start us, length us, event | category | flops | bytes accessed | tf_op | source)
XLA Modules:
  0.0 87.6 jit_solution(13572674770007580372)
XLA Ops:
  1.3 84.3 %gated_attention.1 = bf16[1,64,5120]{2,1,0:T(8,128)(2,1)} custom-call(s32[1]{0:T(128)S(6)} %copy.11.len_ref, s32[1]{0:T(128)S(6)} %copy.12.step_ref, bf16[1,64,5120]{2,1,0:T(8,128)(2,1)} %q_hbm.1, bf16[1,64,5120]{2,1,0:T(8,128)(2,1)} %k_hbm.1, bf16[1,64,5120]{2,1,0:T(8,128)(2,1)} %v_hbm.1, f32[1,5120]{1,0:T(1,128)} %bitcast.4, f32[1,5120]{1,0:T(1,128)} %bitcast.5, ...), custom_call_target="tpu_custom_call" | custom-call | flops 4697620480 | bytes 4194304 | tf_op jit(solution)/shard_map/gated_attention/pallas_call | solution.py:624
  85.6 2.0 %copy.13 = bf16[1,64,5120]{2,1,0:T(8,128)(2,1)} copy(bf16[1,64,5120]{2,1,0:T(8,128)(2,1)} %gated_attention.1) | data formatting | bytes 1310720

commit v5 on v4

--- a/solution.py
+++ b/solution.py
@@ -589,17 +589,31 @@
     give = [rc(tokens(i, oc), out_cols(row), fins.at[i], finr.at[i], other)
             for i, row in enumerate((my_row, pair_row))]
     lax.fori_loop(0, GROUPS + LAST_LAG - 1, step, 0)
+    near_half = zh // 2
+
+    def finish_own(half):
+        for b in range(5):
+            here = pl.ds(al((half * 5 + b) * 128, 128), 128)
+            ob[0, :, here] = (ft[here, :].T * gate_row[0, :, here]).astype(BF)
+
+    def finish_pair(half):
+        for b in range(5):
+            here = pl.ds(al((half * 5 + b) * 128, 128), 128)
+            ob[1, :, here] = pair_in[here, :].T
+
+    def pair_here(p):
+        got(pair_in.at[pl.ds(al(zh_of(p) * GC, 32), GC), :], psr.at[p])
+
+    finish_own(near_half)
+    for p in range(3):
+        pair_here(p)
+    finish_pair(near_half)
     stage_c(GROUPS - 1)
-    for b in range(10):
-        here = slice(b * 128, b * 128 + 128)
-        ob[0, :, here] = (ft[here, :].T * gate_row[0, :, here]).astype(BF)
+    finish_own(1 - near_half)
     keep[0].start()
     give[0].start()
-    for p in range(4):
-        got(pair_in.at[pl.ds(al(zh_of(p) * GC, 32), GC), :], psr.at[p])
-    for b in range(10):
-        here = slice(b * 128, b * 128 + 128)
-        ob[1, :, here] = pair_in[here, :].T
+    pair_here(3)
+    finish_pair(1 - near_half)
     keep[1].start()
     give[1].start()
 

time: 87.8 us -> 87.7 us (level)
  no operation moved by 1% of the time
where the time goes in v5:
time: 87.7 us; the launch traced here: 87.6 us
  Pallas kernels  84.3 us (96%)
  local copies, waits for them, and re-layouts  1.97 us (2%)
  between operations  1.3 us (1%)
    pallas_call x1, Pallas kernels, body(): pl.pallas_call(kernel, out_shape=jax.ShapeDtypeStruct((1, TOK, D), BF), i...  84.3 us
    unnamed x1, local copies, waits for them, and re-layouts  1.97 us

profile of v5, /device:TPU:1, one launch (start us, length us, event | category | flops | bytes accessed | tf_op | source)
XLA Modules:
  0.0 87.6 jit_solution(4980301564784448710)
XLA Ops:
  1.3 84.3 %gated_attention.1 = bf16[1,64,5120]{2,1,0:T(8,128)(2,1)} custom-call(s32[1]{0:T(128)S(6)} %copy.11.len_ref, s32[1]{0:T(128)S(6)} %copy.12.step_ref, bf16[1,64,5120]{2,1,0:T(8,128)(2,1)} %q_hbm.1, bf16[1,64,5120]{2,1,0:T(8,128)(2,1)} %k_hbm.1, bf16[1,64,5120]{2,1,0:T(8,128)(2,1)} %v_hbm.1, f32[1,5120]{1,0:T(1,128)} %bitcast.4, f32[1,5120]{1,0:T(1,128)} %bitcast.5, ...), custom_call_target="tpu_custom_call" | custom-call | flops 4697620480 | bytes 4194304 | tf_op jit(solution)/shard_map/gated_attention/pallas_call | solution.py:638
  85.6 2.0 %copy.13 = bf16[1,64,5120]{2,1,0:T(8,128)(2,1)} copy(bf16[1,64,5120]{2,1,0:T(8,128)(2,1)} %gated_attention.1) | data formatting | bytes 1310720
